TPU v7x, 128 devices: a whole 4x4x4 slice. The times are simulated.
128 devices in a mesh: rep: 64 (over z, y, x), shard: 2 (over core).
Axes of the slice: x: 4, y: 4, z: 4, core: 2. Of those that a mesh axis runs over, the one named last changes fastest.
Arguments:
- hidden_in: bfloat16 [16384, 896], P(('rep', 'shard')), may hold values from -6 to 6
- seq_lengths: int32 [64, 2], P('rep'), may hold values from 32 to 224, as said below
- block_owner: int32 [64, 2], P('rep'), may hold values from 0 to 1, each once within a row
- norm_attn: bfloat16 [2, 896], P(None, 'shard'), may hold values from 0.099609375 to 1.8984375
- w_qkv: bfloat16 [2, 896, 1152], P(None, 'shard'), may hold values from -0.1875 to 0.1875
- b_qkv: bfloat16 [2, 1152], P(None, 'shard'), may hold values from -3 to 3
- w_out: bfloat16 [2, 896, 896], P(None, 'shard'), may hold values from -0.75 to 0.75
- norm_mlp: bfloat16 [2, 896], P(None, 'shard'), may hold values from 0.099609375 to 1.8984375
- w_gate_up: bfloat16 [2, 896, 9728], P(None, 'shard'), may hold values from -0.1875 to 0.1875
- w_down: bfloat16 [2, 4864, 896], P(None, 'shard'), may hold values from -0.125 to 0.125
- grad_out: float32 [16384, 896], P(('rep', 'shard')), may hold values from -6 to 6
Outputs:
- hidden_out: bfloat16 [16384, 896], P(('rep', 'shard'))
- grad_in: float32 [16384, 896], P(('rep', 'shard'))
- grad_norm_attn: float32 [2, 896], P(None, 'shard')
- grad_w_qkv: float32 [2, 896, 1152], P(None, 'shard')
- grad_b_qkv: float32 [2, 1152], P(None, 'shard')
- grad_w_out: float32 [2, 896, 896], P(None, 'shard')
- grad_norm_mlp: float32 [2, 896], P(None, 'shard')
- grad_w_gate_up: float32 [2, 896, 9728], P(None, 'shard')
- grad_w_down: float32 [2, 4864, 896], P(None, 'shard')
Inputs may be any that keep to these rules, and one draw needn't show every extreme that they name: `seq_lengths`: each row lists the lengths of the 2 documents of one group's stream in stream order; they sum to 256; one of them is exactly 224, which one is drawn from the seed. `block_owner`: each row is a permutation: device s of group g holds stream positions block_owner[g, s] * 128 onwards, 128 of them.
All inputs are finite; a program needn't handle non-finite values.
Results may differ from a plain program's by a relative error of at most 0.015.
Values may be sent and summed in bfloat16 or wider, within the bound.
No kernel may reach another device: no remote copies, remote signals or barrier semaphores. Data moves between devices by JAX's collectives and lax.ppermute only.
A program may use at most 384 MiB of HBM per device.

v0:
```python
import jax
import jax.numpy as jnp
from jax import lax
from jax.sharding import PartitionSpec as P

HEADS = 14
KV_HEADS = 2
HEAD = 64


epsilon = 1e-06
base_freq = 1000000.0


def rms_scale(values, gain_row):
    return values * lax.rsqrt(jnp.mean(values * values, axis=1, keepdims=True) + epsilon) * gain_row


def rotate(values, cosine, sine_part):
    half_width = values.shape[-1] // 2
    first_half = values[..., :half_width]
    second = values[..., half_width:]
    return jnp.concatenate(
        [first_half * cosine - second * sine_part, second * cosine + first_half * sine_part],
        axis=-1,
    )


def swiglu(gate_part, up_part):
    return jax.nn.silu(gate_part) * up_part


def doc_position(stream, lengths):
    doc_ends = jnp.cumsum(lengths)
    doc_ids = jnp.sum((stream[:, None] >= doc_ends[None, :]).astype(jnp.int32), axis=1)
    starts = jnp.max(jnp.where(doc_ends[None, :] <= stream[:, None], doc_ends[None, :], 0), axis=1)
    return (doc_ids, stream - starts)


def angles(positions, head_size):
    half_width = head_size // 2
    frequency = jnp.power(base_freq, -(jnp.arange(half_width, dtype=jnp.float32) * 2.0 / head_size))
    turned = positions.astype(jnp.float32)[:, None] * frequency[None, :]
    return (jnp.cos(turned)[:, None, :], jnp.sin(turned)[:, None, :])


def contract_rows(left_side, right_side):
    return lax.dot_general(
        left_side, right_side, (((0,), (0,)), ((), ())), preferred_element_type=jnp.float32
    )


def contract_cols(left_side, right_side):
    return lax.dot_general(
        left_side, right_side, (((1,), (1,)), ((), ())), preferred_element_type=jnp.float32
    )


def body(
    hidden_in,
    seq_lengths,
    block_owner,
    norm_attn,
    w_qkv,
    b_qkv,
    w_out,
    norm_mlp,
    w_gate_up,
    w_down,
    grad_out,
):
    tok_rows = hidden_in.shape[0]
    layer_count = norm_attn.shape[0]
    width_q = HEADS * HEAD
    width_k = KV_HEADS * HEAD
    per_group = HEADS // KV_HEADS
    scale_factor = HEAD ** (-0.5)
    lengths = seq_lengths[0]
    owner_row = block_owner[0]
    offsets = jnp.arange(tok_rows, dtype=jnp.int32)
    key_stream = (owner_row[:, None] * tok_rows + offsets[None, :]).reshape(-1)
    my_stream = owner_row[lax.axis_index("shard")] * tok_rows + offsets
    key_docs, key_pos = doc_position(key_stream, lengths)
    my_docs, positions = doc_position(my_stream, lengths)
    allowed = (my_docs[:, None] == key_docs[None, :]) & (key_stream[None, :] <= my_stream[:, None])
    cosine, sine_part = angles(positions, HEAD)
    stacked = (norm_attn, w_qkv, b_qkv, w_out, norm_mlp, w_gate_up, w_down)
    gathered = (
        lax.all_gather(stacked[0], "shard", axis=1, tiled=True),
        lax.all_gather(stacked[1], "shard", axis=1, tiled=True),
        lax.all_gather(stacked[2], "shard", axis=1, tiled=True),
        lax.all_gather(stacked[3], "shard", axis=1, tiled=True),
        lax.all_gather(stacked[4], "shard", axis=1, tiled=True),
        lax.all_gather(stacked[5], "shard", axis=1, tiled=True),
        lax.all_gather(stacked[6], "shard", axis=1, tiled=True),
    )

    def attn_scores(grouped, all_keys):
        raw_scores = (
            jnp.einsum("qcgd,kcd->cgqk", grouped, all_keys, preferred_element_type=jnp.float32)
            * scale_factor
        )
        return jnp.where(allowed, raw_scores, -1e30)

    residual = hidden_in.astype(jnp.float32)
    kept_state = []
    for layer_index in range(layer_count):
        gain_attn, w_proj, b_proj, w_attn_out, gain_mlp, w_gu, w_dn = [
            member[layer_index] for member in gathered
        ]
        ff_width = w_gu.shape[1] // 2
        normed = rms_scale(residual, gain_attn.astype(jnp.float32)).astype(jnp.bfloat16)
        projected = jnp.dot(normed, w_proj, preferred_element_type=jnp.float32) + b_proj.astype(
            jnp.float32
        )
        queries = rotate(projected[:, :width_q].reshape(-1, HEADS, HEAD), cosine, sine_part).astype(
            jnp.bfloat16
        )
        rot_keys = rotate(
            projected[:, width_q : width_q + width_k].reshape(-1, KV_HEADS, HEAD), cosine, sine_part
        ).astype(jnp.bfloat16)
        values = projected[:, width_q + width_k :].astype(jnp.bfloat16)
        key_vals = lax.all_gather(
            jnp.concatenate([rot_keys.reshape(-1, width_k), values], axis=1),
            "shard",
            axis=0,
            tiled=True,
        )
        all_keys = key_vals[:, :width_k].reshape(-1, KV_HEADS, HEAD)
        all_values = key_vals[:, width_k:].reshape(-1, KV_HEADS, HEAD)
        grouped = queries.reshape(-1, KV_HEADS, per_group, HEAD)
        scores = attn_scores(grouped, all_keys)
        row_max = jnp.max(scores, axis=-1, keepdims=True)
        exp_scores = jnp.exp(scores - row_max)
        row_sum = jnp.sum(exp_scores, axis=-1, keepdims=True)
        attn_probs = (exp_scores / row_sum).astype(jnp.bfloat16)
        log_total = row_max + jnp.log(row_sum)
        attn_mixed = (
            jnp.einsum("cgqk,kcd->qcgd", attn_probs, all_values, preferred_element_type=jnp.float32)
            .reshape(-1, width_q)
            .astype(jnp.bfloat16)
        )
        middle = residual + jnp.dot(attn_mixed, w_attn_out, preferred_element_type=jnp.float32)
        normed_mlp = rms_scale(middle, gain_mlp.astype(jnp.float32)).astype(jnp.bfloat16)
        gate_up = jnp.dot(normed_mlp, w_gu, preferred_element_type=jnp.float32)
        hidden = swiglu(gate_up[:, :ff_width], gate_up[:, ff_width:]).astype(jnp.bfloat16)
        kept_state.append(
            (
                residual,
                normed,
                grouped,
                all_keys,
                all_values,
                log_total,
                attn_mixed,
                middle,
                normed_mlp,
                gate_up,
                hidden,
            )
        )
        residual = middle + jnp.dot(hidden, w_dn, preferred_element_type=jnp.float32)
    back_weights = (
        lax.all_gather(stacked[0], "shard", axis=1, tiled=True),
        lax.all_gather(stacked[1], "shard", axis=1, tiled=True),
        lax.all_gather(stacked[2], "shard", axis=1, tiled=True),
        lax.all_gather(stacked[3], "shard", axis=1, tiled=True),
        lax.all_gather(stacked[4], "shard", axis=1, tiled=True),
        lax.all_gather(stacked[5], "shard", axis=1, tiled=True),
        lax.all_gather(stacked[6], "shard", axis=1, tiled=True),
    )
    grad_resid = grad_out
    collected = [None] * layer_count
    for layer_index in reversed(range(layer_count)):
        (
            resid_in,
            normed,
            grouped,
            all_keys,
            all_values,
            log_total,
            attn_mixed,
            middle,
            normed_mlp,
            gate_up,
            hidden,
        ) = kept_state[layer_index]
        gain_attn, w_proj, b_proj, w_attn_out, gain_mlp, w_gu, w_dn = [
            member[layer_index] for member in back_weights
        ]
        ff_width = w_gu.shape[1] // 2
        out_grad = grad_resid.astype(jnp.bfloat16)
        grad_down = contract_rows(hidden, out_grad)
        grad_hidden = contract_cols(out_grad, w_dn)
        unused_out, swiglu_pull = jax.vjp(swiglu, gate_up[:, :ff_width], gate_up[:, ff_width:])
        grad_gate, grad_up = swiglu_pull(grad_hidden)
        grad_gu = jnp.concatenate([grad_gate, grad_up], axis=1).astype(jnp.bfloat16)
        grad_wgu = contract_rows(normed_mlp, grad_gu)
        grad_normed_mlp = contract_cols(grad_gu, w_gu)
        unused_out, norm_pull = jax.vjp(rms_scale, middle, gain_mlp.astype(jnp.float32))
        grad_mid_norm, grad_gain_mlp = norm_pull(grad_normed_mlp)
        grad_middle = grad_resid + grad_mid_norm
        branch_grad = grad_middle.astype(jnp.bfloat16)
        grad_wo = contract_rows(attn_mixed, branch_grad)
        grad_mixed = (
            contract_cols(branch_grad, w_attn_out)
            .astype(jnp.bfloat16)
            .reshape(-1, KV_HEADS, per_group, HEAD)
        )
        scores = attn_scores(grouped, all_keys)
        probs_full = jnp.where(allowed, jnp.exp(scores - log_total), 0.0)
        grad_probs = jnp.einsum(
            "qcgd,kcd->cgqk", grad_mixed, all_values, preferred_element_type=jnp.float32
        )
        grad_values = jnp.einsum(
            "cgqk,qcgd->kcd",
            probs_full.astype(jnp.bfloat16),
            grad_mixed,
            preferred_element_type=jnp.float32,
        )
        row_dot = jnp.sum(probs_full * grad_probs, axis=-1, keepdims=True)
        grad_scores = (probs_full * (grad_probs - row_dot)).astype(jnp.bfloat16)
        grad_queries = (
            jnp.einsum("cgqk,kcd->qcgd", grad_scores, all_keys, preferred_element_type=jnp.float32)
            * scale_factor
        )
        grad_keys = (
            jnp.einsum("cgqk,qcgd->kcd", grad_scores, grouped, preferred_element_type=jnp.float32)
            * scale_factor
        )
        key_terms = jnp.concatenate(
            [grad_keys.reshape(-1, width_k), grad_values.reshape(-1, width_k)], axis=1
        )
        own_keys = lax.psum_scatter(
            key_terms.astype(jnp.bfloat16), "shard", scatter_dimension=0, tiled=True
        ).astype(jnp.float32)
        grad_q_pre = rotate(grad_queries.reshape(-1, HEADS, HEAD), cosine, -sine_part).reshape(
            -1, width_q
        )
        grad_k_pre = rotate(
            own_keys[:, :width_k].reshape(-1, KV_HEADS, HEAD), cosine, -sine_part
        ).reshape(-1, width_k)
        grad_proj = jnp.concatenate([grad_q_pre, grad_k_pre, own_keys[:, width_k:]], axis=1).astype(
            jnp.bfloat16
        )
        grad_wq = contract_rows(normed, grad_proj)
        grad_bias = jnp.sum(grad_proj.astype(jnp.float32), axis=0)
        grad_normed = contract_cols(grad_proj, w_proj)
        unused_out, norm_pull = jax.vjp(rms_scale, resid_in, gain_attn.astype(jnp.float32))
        grad_in_norm, grad_gain_attn = norm_pull(grad_normed)
        grad_resid = grad_middle + grad_in_norm
        owned = (
            lax.psum_scatter(
                grad_gain_attn.astype(jnp.bfloat16), "shard", scatter_dimension=0, tiled=True
            ).astype(jnp.float32),
            lax.psum_scatter(
                grad_wq.astype(jnp.bfloat16), "shard", scatter_dimension=0, tiled=True
            ).astype(jnp.float32),
            lax.psum_scatter(
                grad_bias.astype(jnp.bfloat16), "shard", scatter_dimension=0, tiled=True
            ).astype(jnp.float32),
            lax.psum_scatter(
                grad_wo.astype(jnp.bfloat16), "shard", scatter_dimension=0, tiled=True
            ).astype(jnp.float32),
            lax.psum_scatter(
                grad_gain_mlp.astype(jnp.bfloat16), "shard", scatter_dimension=0, tiled=True
            ).astype(jnp.float32),
            lax.psum_scatter(
                grad_wgu.astype(jnp.bfloat16), "shard", scatter_dimension=0, tiled=True
            ).astype(jnp.float32),
            lax.psum_scatter(
                grad_down.astype(jnp.bfloat16), "shard", scatter_dimension=0, tiled=True
            ).astype(jnp.float32),
        )
        collected[layer_index] = lax.psum(
            (owned[0], owned[1], owned[2], owned[3], owned[4], owned[5], owned[6]), "rep"
        )
    results = [
        jnp.stack([collected[index][member] for index in range(layer_count)]) for member in range(7)
    ]
    return (
        residual.astype(jnp.bfloat16),
        grad_resid,
        results[0],
        results[1],
        results[2],
        results[3],
        results[4],
        results[5],
        results[6],
    )


def solution(mesh):
    placed = (
        P(("rep", "shard"), None),
        P("rep", None),
        P("rep", None),
        P(None, "shard"),
        P(None, "shard", None),
        P(None, "shard"),
        P(None, "shard", None),
        P(None, "shard"),
        P(None, "shard", None),
        P(None, "shard", None),
        P(("rep", "shard"), None),
    )
    return jax.shard_map(
        body,
        mesh=mesh,
        in_specs=placed,
        out_specs=(
            P(("rep", "shard"), None),
            P(("rep", "shard"), None),
            P(None, "shard"),
            P(None, "shard", None),
            P(None, "shard"),
            P(None, "shard", None),
            P(None, "shard"),
            P(None, "shard", None),
            P(None, "shard", None),
        ),
        check_vma=False,
    )
```

profile of v0, /device:TPU:1, one launch (start us, length us, event | category | flops | bytes accessed | tf_op | source)
XLA Modules:
  0.0 1017.8 jit_solution(18171204116703531871)
XLA Ops:
  22.1 7.6 all-gather.8.cloned.1.call-done
  35.8 11.7 %all-gather.10.cloned.1.call-done = bf16[2,896,896]{2,1,0:T(8,128)(2,1)} async-done(((bf16[2,448,896]{2,1,0:T(8,128)(2,1)}), bf16[2,896,896]{2,1,0:T(8,128)(2,1)}) %all-gather.10.cloned.1.call-update) | async-done | bytes 3211280 | tf_op jit(solution)/shard_map/all_gather | solution.py:92
  50.3 58.8 %all-gather.12.cloned.1.call-done = bf16[2,896,9728]{2,1,0:T(8,128)(2,1)} async-done(((bf16[2,448,9728]{2,1,0:T(8,128)(2,1)}), bf16[2,896,9728]{2,1,0:T(8,128)(2,1)}) %all-gather.12.cloned.1.call-update) | async-done | bytes 34865168 | tf_op jit(solution)/shard_map/all_gather | solution.py:94
  109.1 7.5 fusion.1
  119.6 28.3 %all-gather.14.cloned.1.call-done = bf16[2,4864,896]{2,1,0:T(8,128)(2,1)} async-done(((bf16[2,2432,896]{2,1,0:T(8,128)(2,1)}), bf16[2,4864,896]{2,1,0:T(8,128)(2,1)}) %all-gather.14.cloned.1.call-update) | async-done | bytes 17432592 | tf_op jit(solution)/shard_map/all_gather | solution.py:95
  164.8 7.7 fusion.3
  172.5 8.2 fusion.10
  180.7 13.5 %multiply_reduce_fusion = (bf16[896]{0:T(1024)(128)(2,1)}, f32[128]{0:T(128)S(1)}, f32[128,896]{1,0:T(8,128)}) fusion(f32[128,896]{1,0:T(8,128)S(1)} %get-tuple-element.86, f32[128]{0:T(128)S(1)} %fusion.86, f32[896]{0:T(1024)S(1)} %copy-done.60, bf16[2,896,9728]{2,1,0:T(8,128)(2,1)} %all-gather.12.cloned.1.call-done, ...), kind=kOutput, calls=%fused_computation.129 | convolution fusion | flops 2237037568 | bytes 20846848 | tf_op jit(solution)/shard_map/dot_general | solution.py:54
  205.2 10.3 %reduce-scatter.31.cloned.1.call-done = bf16[128,256]{1,0:T(8,128)(2,1)} async-done(((bf16[256,256]{1,0:T(8,128)(2,1)}), bf16[128,256]{1,0:T(8,128)(2,1)}) %reduce-scatter.31.cloned.1.call-update) | async-done | bytes 65552
  222.6 9.1 fusion.13
  231.8 12.1 %multiply_reduce_fusion.1 = (bf16[896]{0:T(1024)(128)(2,1)}, f32[128]{0:T(128)S(1)}, f32[128,896]{1,0:T(8,128)S(1)}) fusion(f32[128,896]{1,0:T(8,128)S(1)} %get-tuple-element.80, f32[128]{0:T(128)S(1)} %copy-done.79, f32[896]{0:T(1024)S(1)} %copy-done.58, bf16[2,896,9728]{2,1,0:T(8,128)(2,1)} %all-gather.12.cloned.1.call-done, ...), kind=kOutput, calls=%fused_computation.130 | convolution fusion | flops 2237037568 | bytes 20846848 | tf_op jit(solution)/shard_map/dot_general | solution.py:54
  279.7 12.5 %convolution_convert_fusion = bf16[896,9728]{1,0:T(8,128)(2,1)} fusion(bf16[128,4864]{1,0:T(8,128)(2,1)} %get-tuple-element.48, bf16[128,4864]{1,0:T(8,128)(2,1)S(1)} %copy-done.32, f32[128,896]{1,0:T(8,128)S(1)} %copy-done.9, f32[896]{0:T(1024)S(1)} %copy-done.61, f32[128]{0:T(128)S(1)} %copy-done.82), kind=kOutput, calls=%fused_computation.1 | convolution fusion | flops 2245410816 | bytes 20385792 | tf_op jit(solution)/shard_map/dot_general | solution.py:48
  293.7 12.5 %convolution_convert_fusion.1 = bf16[896,9728]{1,0:T(8,128)(2,1)} fusion(bf16[128,4864]{1,0:T(8,128)(2,1)} %get-tuple-element.46, bf16[128,4864]{1,0:T(8,128)(2,1)S(1)} %copy-done.33, f32[128,896]{1,0:T(8,128)S(1)} %copy-done.11, f32[896]{0:T(1024)S(1)} %copy-done.59, f32[128]{0:T(128)S(1)} %copy-done.80), kind=kOutput, calls=%fused_computation.2 | convolution fusion | flops 2245410816 | bytes 20385792 | tf_op jit(solution)/shard_map/dot_general | solution.py:48
  314.2 12.9 %reduce-scatter.15.cloned.1.call-done = bf16[448,1152]{1,0:T(8,128)(2,1)} async-done(((bf16[896,1152]{1,0:T(8,128)(2,1)}), bf16[448,1152]{1,0:T(8,128)(2,1)}) %reduce-scatter.15.cloned.1.call-update) | async-done | bytes 1032208 | tf_op jit(solution)/shard_map/reduce_scatter | solution.py:256
  329.8 20.9 %reduce-scatter.29.cloned.1.call-done = bf16[2432,896]{1,0:T(8,128)(2,1)} async-done(((bf16[4864,896]{1,0:T(8,128)(2,1)}), bf16[2432,896]{1,0:T(8,128)(2,1)}) %reduce-scatter.29.cloned.1.call-update) | async-done | bytes 4358160 | tf_op jit(solution)/shard_map/reduce_scatter | solution.py:271
  356.8 17.5 %reduce-scatter.27.cloned.1.call-done = bf16[2432,896]{1,0:T(8,128)(2,1)} async-done(((bf16[4864,896]{1,0:T(8,128)(2,1)}), bf16[2432,896]{1,0:T(8,128)(2,1)}) %reduce-scatter.27.cloned.1.call-update) | async-done | bytes 4358160 | tf_op jit(solution)/shard_map/reduce_scatter | solution.py:271
  380.5 27.7 %reduce-scatter.25.cloned.1.call-done = bf16[448,9728]{1,0:T(8,128)(2,1)} async-done(((bf16[896,9728]{1,0:T(8,128)(2,1)}), bf16[448,9728]{1,0:T(8,128)(2,1)}) %reduce-scatter.25.cloned.1.call-update) | async-done | bytes 8716304 | tf_op jit(solution)/shard_map/reduce_scatter | solution.py:268
  408.2 12.0 %bitcast_convert_fusion = f32[1,448,9728]{2,1,0:T(8,128)} fusion(bf16[448,9728]{1,0:T(8,128)(2,1)} %reduce-scatter.25.cloned.1.call-done), kind=kLoop, calls=%fused_computation.14 | loop fusion | flops 4358144 | bytes 26148864 | tf_op jit(solution)/shard_map/stack | solution.py:279
  420.2 21.8 %reduce-scatter.23.cloned.1.call-done = bf16[448,9728]{1,0:T(8,128)(2,1)} async-done(((bf16[896,9728]{1,0:T(8,128)(2,1)}), bf16[448,9728]{1,0:T(8,128)(2,1)}) %reduce-scatter.23.cloned.1.call-update) | async-done | bytes 8716304 | tf_op jit(solution)/shard_map/reduce_scatter | solution.py:268
  442.0 12.0 %bitcast_convert_fusion.1 = f32[1,448,9728]{2,1,0:T(8,128)} fusion(bf16[448,9728]{1,0:T(8,128)(2,1)} %reduce-scatter.23.cloned.1.call-done), kind=kLoop, calls=%fused_computation.15 | loop fusion | flops 4358144 | bytes 26148864 | tf_op jit(solution)/shard_map/stack | solution.py:279
  467.5 302.9 %all-reduce.6 = (f32[1,448]{1,0:T(1,128)S(1)}, f32[1,448]{1,0:T(1,128)S(1)}, f32[1,576]{1,0:T(1,128)S(1)}, f32[1,576]{1,0:T(1,128)S(1)}, f32[1,448]{1,0:T(1,128)S(1)}, /*index=5*/f32[1,448]{1,0:T(1,128)S(1)}) all-reduce(f32[1,448]{1,0:T(1,128)S(1)} %bitcast.309, ...), channel_id=1, replica_groups=mesh['rep'=64,'shard'=2] {'rep'}, use_global_device_ids=true, to_apply=%region_25.26 | all-reduce | flops 2944 | bytes 23552 | tf_op jit(solution)/shard_map/psum | solution.py:275
  773.1 197.4 %all-reduce.11.cloned.1.call-done = (f32[1,448,1152]{2,1,0:T(8,128)}, f32[1,448,1152]{2,1,0:T(8,128)}, f32[1,448,896]{2,1,0:T(8,128)}, f32[1,448,896]{2,1,0:T(8,...) async-done(((f32[1,448,1152]{2,1,0:T(8,128)}, f32[1,448,1152]{2,1,0:T(8,128)}, ...) | async-done | bytes 59637776 | tf_op jit(solution)/shard_map/psum | solution.py:275
  977.1 13.6 %pad_maximum_fusion.1 = f32[2,2432,896]{2,1,0:T(8,128)} fusion(f32[1,2432,896]{2,1,0:T(8,128)} %get-tuple-element.37, f32[1,2432,896]{2,1,0:T(8,128)} %get-tuple-element.38), kind=kLoop, calls=%fused_computation.5 | loop fusion | flops 4358144 | bytes 34865152 | tf_op jit(solution)/shard_map/stack | solution.py:279
  999.1 11.7 %pad_maximum_fusion = f32[2,448,9728]{2,1,0:T(8,128)} fusion(f32[1,448,9728]{2,1,0:T(8,128)S(1)} %bitcast.255, f32[1,448,9728]{2,1,0:T(8,128)S(1)} %copy-done), kind=kLoop, calls=%fused_computation | loop fusion | flops 8716288 | bytes 69730304 | tf_op jit(solution)/shard_map/stack | solution.py:279
  (394 shorter events, 150.3 us)
Async XLA Ops:
  7.2 22.4 %all-gather.8.cloned.1.call-start = ((), (), s32[]{:S(2)}) async-start(), calls=%async_computation.10 | async-start | bytes 6193152 | tf_op jit(solution)/shard_map/all_gather | solution.py:90
  7.9 39.7 %all-gather.10.cloned.1.call-start = ((), (), s32[]{:S(2)}) async-start(), calls=%async_computation.11 | async-start | bytes 4816896 | tf_op jit(solution)/shard_map/all_gather | solution.py:92
  8.7 100.4 %all-gather.12.cloned.1.call-start = ((), (), s32[]{:S(2)}) async-start(), calls=%async_computation.12 | async-start | bytes 52297728 | tf_op jit(solution)/shard_map/all_gather | solution.py:94
  9.5 138.4 %all-gather.14.cloned.1.call-start = ((), (), s32[]{:S(2)}) async-start(), calls=%async_computation.13 | async-start | bytes 26148864 | tf_op jit(solution)/shard_map/all_gather | solution.py:95
  10.0 205.5 %reduce-scatter.31.cloned.1.call-start = ((), (), s32[]{:S(2)}) async-start(), calls=%async_computation.22 | async-start | bytes 196608
  18.9 90.2 %copy-start.57 = (f32[896]{0:T(1024)}, f32[896]{0:T(1024)S(1)}, u32[]{:S(2)}) copy-start(f32[896]{0:T(1024)S(1)} %get-tuple-element.20) | copy-start | bytes 10756
  35.8 73.3 %copy-start.36 = (bf16[2,64,7,128]{3,1,2,0:T(8,128)(2,1)}, bf16[2,64,7,128]{3,1,2,0:T(8,128)(2,1)S(1)}, u32[]{:S(2)}) copy-start(bf16[2,64,7,128]{3,1,2,0:T(8,128)(2,1)S(1)} %convolution_convert_fusion.9) | copy-start | bytes 688132
  49.5 59.5 %copy-start.96 = (f32[128]{0:T(128)}, f32[128]{0:T(128)S(1)}, u32[]{:S(2)}) copy-start(f32[128]{0:T(128)S(1)} %get-tuple-element.79) | copy-start | bytes 1540
  49.5 182.2 %copy-start.10 = (f32[128,896]{1,0:T(8,128)}, f32[128,896]{1,0:T(8,128)S(1)}, u32[]{:S(2)}) copy-start(f32[128,896]{1,0:T(8,128)S(1)} %get-tuple-element.80) | copy-start | bytes 1376260
  49.6 59.5 %copy-start.78 = (f32[128]{0:T(128)}, f32[128]{0:T(128)S(1)}, u32[]{:S(2)}) copy-start(f32[128]{0:T(128)S(1)} %fusion.84) | copy-start | bytes 1540
  119.5 33.4 %copy-start.5 = (bf16[128,4864]{1,0:T(8,128)(2,1)}, bf16[128,4864]{1,0:T(8,128)(2,1)S(1)}, u32[]{:S(2)}) copy-start(bf16[128,4864]{1,0:T(8,128)(2,1)S(1)} %multiply_convert_fusion.3) | copy-start | bytes 3735556
  164.8 29.4 %copy-start.8 = (f32[128,896]{1,0:T(8,128)}, f32[128,896]{1,0:T(8,128)S(1)}, u32[]{:S(2)}) copy-start(f32[128,896]{1,0:T(8,128)S(1)} %get-tuple-element.86) | copy-start | bytes 1376260
  164.8 29.4 %copy-start.81 = (f32[128]{0:T(128)}, f32[128]{0:T(128)S(1)}, u32[]{:S(2)}) copy-start(f32[128]{0:T(128)S(1)} %fusion.86) | copy-start | bytes 1540
  203.8 59.1 %reduce-scatter.33.cloned.1.call-start = ((), (), s32[]{:S(2)}) async-start(), calls=%async_computation.23 | async-start | bytes 196608
  251.2 55.3 %reduce-scatter.21.cloned.1.call-start = ((), (), s32[]{:S(2)}) async-start(), calls=%async_computation.17 | async-start | bytes 2408448 | tf_op jit(solution)/shard_map/reduce_scatter | solution.py:262
  254.1 55.0 %reduce-scatter.19.cloned.1.call-start = ((), (), s32[]{:S(2)}) async-start(), calls=%async_computation.16 | async-start | bytes 2408448 | tf_op jit(solution)/shard_map/reduce_scatter | solution.py:262
  256.0 55.6 %reduce-scatter.17.cloned.1.call-start = ((), (), s32[]{:S(2)}) async-start(), calls=%async_computation.15 | async-start | bytes 3096576 | tf_op jit(solution)/shard_map/reduce_scatter | solution.py:256
  258.2 68.9 %reduce-scatter.15.cloned.1.call-start = ((), (), s32[]{:S(2)}) async-start(), calls=%async_computation.14 | async-start | bytes 3096576 | tf_op jit(solution)/shard_map/reduce_scatter | solution.py:256
  267.0 83.7 %reduce-scatter.29.cloned.1.call-start = ((), (), s32[]{:S(2)}) async-start(), calls=%async_computation.21 | async-start | bytes 13074432 | tf_op jit(solution)/shard_map/reduce_scatter | solution.py:271
  272.1 102.2 %reduce-scatter.27.cloned.1.call-start = ((), (), s32[]{:S(2)}) async-start(), calls=%async_computation.20 | async-start | bytes 13074432 | tf_op jit(solution)/shard_map/reduce_scatter | solution.py:271
  278.3 129.9 %reduce-scatter.25.cloned.1.call-start = ((), (), s32[]{:S(2)}) async-start(), calls=%async_computation.19 | async-start | bytes 26148864 | tf_op jit(solution)/shard_map/reduce_scatter | solution.py:268
  292.2 149.9 %reduce-scatter.23.cloned.1.call-start = ((), (), s32[]{:S(2)}) async-start(), calls=%async_computation.18 | async-start | bytes 26148864 | tf_op jit(solution)/shard_map/reduce_scatter | solution.py:268
  306.2 664.4 %all-reduce.11.cloned.1.call-start = ((), (), s32[]{:S(2)}) async-start(), calls=%async_computation.24 | async-start | bytes 119275520 | tf_op jit(solution)/shard_map/psum | solution.py:275
  462.5 309.7 %copy-start.95 = (f32[128]{0:T(128)S(1)}, f32[128]{0:T(128)}, u32[]{:S(2)}) copy-start(f32[128]{0:T(128)} %copy-done.94) | copy-start | bytes 1540
  (100 other events, 512.3 us)
Sparse Core Ops, SparseCore 0:
  9.7 19.9 all-gather.7
  31.3 16.2 all-gather.9
  49.3 59.7 all-gather.11
  110.6 37.1 all-gather.13
  204.0 11.5 reduce-scatter.30
  251.3 11.5 reduce-scatter.32
  265.3 13.0 reduce-scatter.20
  280.8 13.1 reduce-scatter.18
  296.9 13.6 reduce-scatter.16
  313.4 13.6 reduce-scatter.14
  329.5 21.0 reduce-scatter.28
  353.1 21.1 reduce-scatter.26
  377.3 30.8 reduce-scatter.24
  411.2 30.8 reduce-scatter.22
  454.2 516.2 all-reduce.10
where the time goes:
time: 1030 us; the launch traced here: 1020 us
  waiting for transfers between devices  422 us (41%)
  blocking collectives  317 us (31%)
  matrix products  135 us (13%)
  other arithmetic  96.9 us (9%)
  local copies, waits for them, and re-layouts  28.7 us (3%)
  between operations  17.3 us (2%)
    psum x1, blocking collectives, body(): lax.psum((owned[0], owned[1], owned[2], owned[3], owned[4], owned[5], own...  303 us
    psum x1, waiting for transfers between devices, body(): lax.psum((owned[0], owned[1], owned[2], owned[3], owned[4], owned[5], own...  197 us
    another operation x15, other arithmetic, body(): jnp.stack([collected[index][member] for index in range(layer_count)])  80.2 us
    all_gather x1, waiting for transfers between devices, body(): lax.all_gather(stacked[5], 'shard', axis=1, tiled=True)  58.8 us
    dot_general x8, matrix products, contract_cols(): lax.dot_general(left_side, right_side, (((1,), (1,)), ((), ())), preferre...  51 us
    reduce_scatter x2, waiting for transfers between devices, body(): lax.psum_scatter(grad_wgu.astype(jnp.bfloat16), 'shard', scatter_dimensio...  49.6 us
    dot_general x8, matrix products, contract_rows(): lax.dot_general(left_side, right_side, (((0,), (0,)), ((), ())), preferre...  44.1 us
    reduce_scatter x2, waiting for transfers between devices, body(): lax.psum_scatter(grad_down.astype(jnp.bfloat16), 'shard', scatter_dimensi...  38.4 us
  transfers between devices with their start and end apart: 15, of which 12 were waited for; matrix products, arithmetic and copies ran while one was open for 11% of the time, Pallas kernels for 0%

commit v1 on v0

v1 whole, which is shorter than its diff:
```python
import functools

import jax
import jax.numpy as jnp
from jax import lax
from jax.experimental import pallas as pl
from jax.experimental.pallas import tpu as pltpu
from jax.sharding import PartitionSpec as P

HEADS = 14
KV_HEADS = 2
HEAD = 64
D = 896
HALF = 448
FF = 4864
FH = 2432
QKV = 1152
TOK = 128

epsilon = 1e-06
base_freq = 1000000.0
VMEM = 60 * 1024 * 1024
F32 = jnp.float32
BF = jnp.bfloat16


def rms_scale(values, gain_row):
    return values * lax.rsqrt(jnp.mean(values * values, axis=1, keepdims=True) + epsilon) * gain_row


def rotate(values, cosine, sine_part):
    half_width = values.shape[-1] // 2
    first_half = values[..., :half_width]
    second = values[..., half_width:]
    return jnp.concatenate(
        [first_half * cosine - second * sine_part, second * cosine + first_half * sine_part],
        axis=-1,
    )


def doc_position(stream, lengths):
    doc_ends = jnp.cumsum(lengths)
    doc_ids = jnp.sum((stream[:, None] >= doc_ends[None, :]).astype(jnp.int32), axis=1)
    starts = jnp.max(jnp.where(doc_ends[None, :] <= stream[:, None], doc_ends[None, :], 0), axis=1)
    return (doc_ids, stream - starts)


def angles(positions, head_size):
    half_width = head_size // 2
    frequency = jnp.power(base_freq, -(jnp.arange(half_width, dtype=F32) * 2.0 / head_size))
    turned = positions.astype(F32)[:, None] * frequency[None, :]
    return (jnp.cos(turned)[:, None, :], jnp.sin(turned)[:, None, :])


def contract_rows(left_side, right_side):
    return lax.dot_general(
        left_side, right_side, (((0,), (0,)), ((), ())), preferred_element_type=F32
    )


def contract_cols(left_side, right_side):
    return lax.dot_general(
        left_side, right_side, (((1,), (1,)), ((), ())), preferred_element_type=F32
    )


def swap(value):
    return lax.ppermute(value, "shard", [(0, 1), (1, 0)])


def mlp_up_kernel(s_ref, bo_ref, bx_ref, go_ref, uo_ref, gx_ref, ux_ref, gate_ref, up_ref, m_ref):
    gate = jnp.dot(bo_ref[...], go_ref[0], preferred_element_type=F32)
    gate += jnp.dot(bx_ref[...], gx_ref[0], preferred_element_type=F32)
    up = jnp.dot(bo_ref[...], uo_ref[0], preferred_element_type=F32)
    up += jnp.dot(bx_ref[...], ux_ref[0], preferred_element_type=F32)
    gate_ref[...] = gate
    up_ref[...] = up
    m_ref[...] = (gate * jax.nn.sigmoid(gate) * up).astype(BF)


def w_specs(layer):
    return [
        pl.BlockSpec((1, HALF, FH), lambda i, s, l=layer: (l, 0, s[0])),
        pl.BlockSpec((1, HALF, FH), lambda i, s, l=layer: (l, 0, 2 + s[0])),
    ]


def whole(shape):
    return pl.BlockSpec(shape, lambda i, s: (0,) * len(shape))


def mlp_up(s, b_own, b_oth, w_own, w_oth, layer):
    rows = b_own.shape[0]
    return pl.pallas_call(
        mlp_up_kernel,
        grid_spec=pltpu.PrefetchScalarGridSpec(
            num_scalar_prefetch=1,
            grid=(1,),
            in_specs=[whole((rows, HALF)), whole((rows, HALF))] + w_specs(layer) + w_specs(0),
            out_specs=[whole((rows, FH)), whole((rows, FH)), whole((rows, FH))],
        ),
        out_shape=[
            jax.ShapeDtypeStruct((rows, FH), F32),
            jax.ShapeDtypeStruct((rows, FH), F32),
            jax.ShapeDtypeStruct((rows, FH), BF),
        ],
        compiler_params=pltpu.CompilerParams(vmem_limit_bytes=VMEM),
        cost_estimate=pl.CostEstimate(
            flops=4 * rows * D * FH, bytes_accessed=14_500_000, transcendentals=rows * FH
        ),
        name="mlp_up",
    )(s, b_own, b_oth, w_own, w_own, w_oth, w_oth)


def mlp_back_kernel(
    s_ref, df_ref, wd_ref, gate_ref, up_ref, go_ref, uo_ref, gx_ref, ux_ref, dgu_ref, dbo_ref, dbx_ref
):
    dm = contract_cols(df_ref[...], wd_ref[0])
    gate = gate_ref[...]
    sig = jax.nn.sigmoid(gate)
    act = gate * sig
    dup = (dm * act).astype(BF)
    dgate = (dm * up_ref[...] * (sig * (1.0 + gate * (1.0 - sig)))).astype(BF)
    dgu_ref[:, :FH] = dgate
    dgu_ref[:, FH:] = dup
    dbo_ref[...] = contract_cols(dgate, go_ref[0]) + contract_cols(dup, uo_ref[0])
    dbx_ref[...] = contract_cols(dgate, gx_ref[0]) + contract_cols(dup, ux_ref[0])


def mlp_back(s, df, w_down, gate, up, w_own, w_oth, layer):
    rows = df.shape[0]
    return pl.pallas_call(
        mlp_back_kernel,
        grid_spec=pltpu.PrefetchScalarGridSpec(
            num_scalar_prefetch=1,
            grid=(1,),
            in_specs=[
                whole((rows, D)),
                pl.BlockSpec((1, FH, D), lambda i, s, l=layer: (l, 0, 0)),
                whole((rows, FH)),
                whole((rows, FH)),
            ]
            + w_specs(layer)
            + w_specs(0),
            out_specs=[whole((rows, 2 * FH)), whole((rows, HALF)), whole((rows, HALF))],
        ),
        out_shape=[
            jax.ShapeDtypeStruct((rows, 2 * FH), BF),
            jax.ShapeDtypeStruct((rows, HALF), F32),
            jax.ShapeDtypeStruct((rows, HALF), F32),
        ],
        compiler_params=pltpu.CompilerParams(vmem_limit_bytes=VMEM),
        cost_estimate=pl.CostEstimate(
            flops=6 * rows * D * FH, bytes_accessed=23_000_000, transcendentals=rows * FH
        ),
        name="mlp_back",
    )(s, df, w_down, gate, up, w_own, w_own, w_oth, w_oth)


def grad_gu_kernel(s_ref, b_ref, own_ref, oth_ref, out_ref):
    mine = lax.rem(pl.program_id(0), 2) == s_ref[0]

    @pl.when(mine)
    def _():
        out_ref[...] = contract_rows(b_ref[0], own_ref[...]).astype(BF)

    @pl.when(jnp.logical_not(mine))
    def _():
        out_ref[...] = contract_rows(b_ref[1], oth_ref[...]).astype(BF)


def grad_gu(s, b_pair, dgu_own, dgu_oth):
    rows = dgu_own.shape[0]
    return pl.pallas_call(
        grad_gu_kernel,
        grid_spec=pltpu.PrefetchScalarGridSpec(
            num_scalar_prefetch=1,
            grid=(4,),
            in_specs=[
                whole((2, rows, HALF)),
                pl.BlockSpec((rows, FH), lambda i, s: (0, i // 2)),
                pl.BlockSpec((rows, FH), lambda i, s: (0, i // 2)),
            ],
            out_specs=pl.BlockSpec((HALF, FH), lambda i, s: (0, i)),
        ),
        out_shape=jax.ShapeDtypeStruct((HALF, 2 * FF), BF),
        compiler_params=pltpu.CompilerParams(vmem_limit_bytes=VMEM),
        cost_estimate=pl.CostEstimate(
            flops=4 * rows * HALF * FF, bytes_accessed=14_000_000, transcendentals=0
        ),
        name="grad_gu",
    )(s, b_pair, dgu_own, dgu_oth)


def body(
    hidden_in,
    seq_lengths,
    block_owner,
    norm_attn,
    w_qkv,
    b_qkv,
    w_out,
    norm_mlp,
    w_gate_up,
    w_down,
    grad_out,
):
    layer_count = 2
    width_q = HEADS * HEAD
    width_k = KV_HEADS * HEAD
    per_group = HEADS // KV_HEADS
    scale_factor = HEAD ** (-0.5)
    me = lax.axis_index("shard")
    first = me == 0
    s_arr = me.astype(jnp.int32).reshape(1)

    def pick(low, high):
        return jnp.where(first, low, high)

    def own_half(value, size):
        return pick(value[..., :size], value[..., size:])

    def other_half(value, size):
        return pick(value[..., size:], value[..., :size])

    def join(mine, theirs, axis):
        return pick(
            jnp.concatenate([mine, theirs], axis=axis), jnp.concatenate([theirs, mine], axis=axis)
        )

    lengths = seq_lengths[0]
    owner_row = block_owner[0]
    offsets = jnp.arange(TOK, dtype=jnp.int32)
    my_stream = owner_row[me] * TOK + offsets
    key_stream = jnp.concatenate([my_stream, owner_row[1 - me] * TOK + offsets])
    key_docs, key_pos = doc_position(key_stream, lengths)
    my_docs, positions = doc_position(my_stream, lengths)
    allowed = (my_docs[:, None] == key_docs[None, :]) & (key_stream[None, :] <= my_stream[:, None])
    cosine, sine_part = angles(positions, HEAD)

    small_own = jnp.concatenate([norm_attn, b_qkv, norm_mlp], axis=1)
    small_oth = swap(small_own)
    gains_attn = join(small_own[:, :HALF], small_oth[:, :HALF], 1).astype(F32)
    biases = join(small_own[:, HALF:-HALF], small_oth[:, HALF:-HALF], 1).astype(F32)
    gains_mlp = join(small_own[:, -HALF:], small_oth[:, -HALF:], 1).astype(F32)
    w_proj, w_attn_out, w_gu_oth = [], [], []
    for layer in range(layer_count):
        w_proj.append(join(w_qkv[layer], swap(w_qkv[layer]), 0))
        w_attn_out.append(join(w_out[layer], swap(w_out[layer]), 0))
        w_gu_oth.append(swap(w_gate_up[layer : layer + 1]))

    def attn_scores(grouped, all_keys):
        raw_scores = (
            jnp.einsum("qcgd,kcd->cgqk", grouped, all_keys, preferred_element_type=F32)
            * scale_factor
        )
        return jnp.where(allowed, raw_scores, -1e30)

    residual = hidden_in.astype(F32)
    kept_state = []
    for layer in range(layer_count):
        normed = rms_scale(residual, gains_attn[layer]).astype(BF)
        normed_oth = swap(other_half(normed, HALF))
        projected = jnp.dot(normed, w_proj[layer], preferred_element_type=F32) + biases[layer]
        queries = rotate(projected[:, :width_q].reshape(-1, HEADS, HEAD), cosine, sine_part).astype(
            BF
        )
        rot_keys = rotate(
            projected[:, width_q : width_q + width_k].reshape(-1, KV_HEADS, HEAD), cosine, sine_part
        ).astype(BF)
        values = projected[:, width_q + width_k :].astype(BF)
        kv = jnp.concatenate([rot_keys.reshape(-1, width_k), values], axis=1)
        key_vals = jnp.concatenate([kv, swap(kv)], axis=0)
        all_keys = key_vals[:, :width_k].reshape(-1, KV_HEADS, HEAD)
        all_values = key_vals[:, width_k:].reshape(-1, KV_HEADS, HEAD)
        grouped = queries.reshape(-1, KV_HEADS, per_group, HEAD)
        scores = attn_scores(grouped, all_keys)
        row_max = jnp.max(scores, axis=-1, keepdims=True)
        exp_scores = jnp.exp(scores - row_max)
        row_sum = jnp.sum(exp_scores, axis=-1, keepdims=True)
        attn_probs = (exp_scores / row_sum).astype(BF)
        log_total = row_max + jnp.log(row_sum)
        attn_mixed = (
            jnp.einsum("cgqk,kcd->qcgd", attn_probs, all_values, preferred_element_type=F32)
            .reshape(-1, width_q)
            .astype(BF)
        )
        mixed_oth = swap(other_half(attn_mixed, HALF))
        middle = residual + jnp.dot(attn_mixed, w_attn_out[layer], preferred_element_type=F32)
        normed_mlp = rms_scale(middle, gains_mlp[layer]).astype(BF)
        normed_cat = jnp.concatenate([normed_mlp, swap(normed_mlp)], axis=0)
        b_own = own_half(normed_cat, HALF)
        b_oth = other_half(normed_cat, HALF)
        gate, up, hidden = mlp_up(s_arr, b_own, b_oth, w_gate_up, w_gu_oth[layer], layer)
        partial = jnp.dot(hidden, w_down[layer], preferred_element_type=F32)
        kept_state.append(
            (
                residual,
                normed,
                normed_oth,
                grouped,
                all_keys,
                all_values,
                log_total,
                attn_mixed,
                mixed_oth,
                middle,
                b_own,
                gate,
                up,
                hidden,
            )
        )
        residual = middle + partial[:TOK] + swap(partial[TOK:])

    grad_resid = grad_out
    collected = [None] * layer_count
    for layer in reversed(range(layer_count)):
        (
            resid_in,
            normed,
            normed_oth,
            grouped,
            all_keys,
            all_values,
            log_total,
            attn_mixed,
            mixed_oth,
            middle,
            b_own,
            gate,
            up,
            hidden,
        ) = kept_state[layer]
        out_grad = grad_resid.astype(BF)
        out_cat = jnp.concatenate([out_grad, swap(out_grad)], axis=0)
        dgu, db_own, db_oth = mlp_back(
            s_arr, out_cat, w_down, gate, up, w_gate_up, w_gu_oth[layer], layer
        )
        grad_down = contract_rows(hidden, out_cat).astype(BF)
        dgu_oth = swap(dgu)
        b_pair = jnp.stack([b_own, jnp.concatenate([b_own[TOK:], b_own[:TOK]], axis=0)])
        grad_wgu = grad_gu(s_arr, b_pair, dgu, dgu_oth)
        db = join(db_own, db_oth, 1)
        grad_normed_mlp = db[:TOK] + swap(db[TOK:])
        unused_out, norm_pull = jax.vjp(rms_scale, middle, gains_mlp[layer])
        grad_mid_norm, grad_gain_mlp = norm_pull(grad_normed_mlp)
        grad_middle = grad_resid + grad_mid_norm
        branch_grad = grad_middle.astype(BF)
        branch_cat = jnp.concatenate([branch_grad, swap(branch_grad)], axis=0)
        mixed_cat = jnp.concatenate([own_half(attn_mixed, HALF), mixed_oth], axis=0)
        grad_wo = contract_rows(mixed_cat, branch_cat).astype(BF)
        grad_mixed = (
            contract_cols(branch_grad, w_attn_out[layer])
            .astype(BF)
            .reshape(-1, KV_HEADS, per_group, HEAD)
        )
        scores = attn_scores(grouped, all_keys)
        probs_full = jnp.where(allowed, jnp.exp(scores - log_total), 0.0)
        grad_probs = jnp.einsum(
            "qcgd,kcd->cgqk", grad_mixed, all_values, preferred_element_type=F32
        )
        grad_values = jnp.einsum(
            "cgqk,qcgd->kcd", probs_full.astype(BF), grad_mixed, preferred_element_type=F32
        )
        row_dot = jnp.sum(probs_full * grad_probs, axis=-1, keepdims=True)
        grad_scores = (probs_full * (grad_probs - row_dot)).astype(BF)
        grad_queries = (
            jnp.einsum("cgqk,kcd->qcgd", grad_scores, all_keys, preferred_element_type=F32)
            * scale_factor
        )
        grad_keys = (
            jnp.einsum("cgqk,qcgd->kcd", grad_scores, grouped, preferred_element_type=F32)
            * scale_factor
        )
        key_terms = jnp.concatenate(
            [grad_keys.reshape(-1, width_k), grad_values.reshape(-1, width_k)], axis=1
        )
        own_keys = key_terms[:TOK] + swap(key_terms[TOK:])
        grad_q_pre = rotate(grad_queries.reshape(-1, HEADS, HEAD), cosine, -sine_part).reshape(
            -1, width_q
        )
        grad_k_pre = rotate(
            own_keys[:, :width_k].reshape(-1, KV_HEADS, HEAD), cosine, -sine_part
        ).reshape(-1, width_k)
        grad_proj = jnp.concatenate([grad_q_pre, grad_k_pre, own_keys[:, width_k:]], axis=1).astype(
            BF
        )
        proj_cat = jnp.concatenate([grad_proj, swap(grad_proj)], axis=0)
        normed_cat = jnp.concatenate([own_half(normed, HALF), normed_oth], axis=0)
        grad_wq = contract_rows(normed_cat, proj_cat).astype(BF)
        grad_bias = own_half(jnp.sum(proj_cat.astype(F32), axis=0), QKV // 2)
        grad_normed = contract_cols(grad_proj, w_proj[layer])
        unused_out, norm_pull = jax.vjp(rms_scale, resid_in, gains_attn[layer])
        grad_in_norm, grad_gain_attn = norm_pull(grad_normed)
        grad_resid = grad_middle + grad_in_norm
        gains = jnp.stack([grad_gain_attn, grad_gain_mlp])
        gains = own_half(gains, HALF) + swap(other_half(gains, HALF))
        vectors = jnp.concatenate([gains[0], gains[1], grad_bias]).astype(BF)
        collected[layer] = (vectors, grad_wq, grad_wo, grad_wgu, grad_down)
    summed = lax.psum(collected, "rep")
    members = [
        jnp.stack([summed[index][member].astype(F32) for index in range(layer_count)])
        for member in range(5)
    ]
    vectors = members[0]
    return (
        residual.astype(BF),
        grad_resid,
        vectors[:, :HALF],
        members[1],
        vectors[:, 2 * HALF :],
        members[2],
        vectors[:, HALF : 2 * HALF],
        members[3],
        members[4],
    )


def solution(mesh):
    placed = (
        P(("rep", "shard"), None),
        P("rep", None),
        P("rep", None),
        P(None, "shard"),
        P(None, "shard", None),
        P(None, "shard"),
        P(None, "shard", None),
        P(None, "shard"),
        P(None, "shard", None),
        P(None, "shard", None),
        P(("rep", "shard"), None),
    )
    return jax.shard_map(
        body,
        mesh=mesh,
        in_specs=placed,
        out_specs=(
            P(("rep", "shard"), None),
            P(("rep", "shard"), None),
            P(None, "shard"),
            P(None, "shard", None),
            P(None, "shard"),
            P(None, "shard", None),
            P(None, "shard"),
            P(None, "shard", None),
            P(None, "shard", None),
        ),
        check_vma=False,
    )
```

time: 1030 us -> 624 us (0.61)
  the two profiles are of different devices: /device:TPU:1 before, /device:TPU:0 now
where the time goes in v1:
time: 624 us; the launch traced here: 615 us
  blocking collectives  355 us (57%)
  other arithmetic  65.1 us (10%)
  Pallas kernels  58.2 us (9%)
  matrix products  52.2 us (8%)
  local copies, waits for them, and re-layouts  35.1 us (6%)
  waiting for transfers between devices  21.2 us (3%)
  between operations  17.2 us (3%)
  starting transfers between devices  10.4 us (2%)
    psum x1, blocking collectives, body(): summed = lax.psum(collected, 'rep')  355 us
    another operation x5, other arithmetic, body(): jnp.stack([summed[index][member].astype(F32) for index in range(layer_cou...  32.7 us
    pallas_call x2, Pallas kernels, mlp_back(): pl.pallas_call(mlp_back_kernel, grid_spec=pltpu.PrefetchScalarGridSpec(nu...  23.5 us
    ppermute x31, waiting for transfers between devices, swap(): return lax.ppermute(value, 'shard', [(0, 1), (1, 0)])  21.1 us
    pallas_call x2, Pallas kernels, grad_gu(): pl.pallas_call(grad_gu_kernel, grid_spec=pltpu.PrefetchScalarGridSpec(num...  17.6 us
    pallas_call x2, Pallas kernels, mlp_up(): pl.pallas_call(mlp_up_kernel, grid_spec=pltpu.PrefetchScalarGridSpec(num_...  17.1 us
    dot_general x6, matrix products, contract_rows(): lax.dot_general(left_side, right_side, (((0,), (0,)), ((), ())), preferre...  15.7 us
    select_n x10, other arithmetic, pick(): return jnp.where(first, low, high)  13.4 us
  transfers between devices with their start and end apart: 32, of which 10 were waited for; matrix products, arithmetic and copies ran while one was open for 17% of the time, Pallas kernels for 8%

profile of v1, /device:TPU:0, one launch (start us, length us, event | category | flops | bytes accessed | tf_op | source)
XLA Modules:
  0.0 614.8 jit_solution(10705419194774408139)
XLA Ops:
  7.3 11.9 %fusion.113 = (bf16[1,448,9728]{2,1,0:T(8,128)(2,1)}, bf16[1,448,9728]{2,1,0:T(8,128)(2,1)}) fusion(bf16[2,448,9728]{2,1,0:T(8,128)(2,1)} %uo_ref.7), kind=kLoop, calls=%fused_computation.292 | loop fusion | bytes 34865152 | tf_op jit(solution)/shard_map/slice | solution.py:250
  29.3 5.6 collective-permute-done.13
  40.4 9.4 %collective-permute-done.2 = bf16[128,256]{1,0:T(8,128)(2,1)S(1)} collective-permute-done((bf16[128,256]{1,0:T(8,128)(2,1)S(1)}, bf16[128,256]{1,0:T(8,128)(2,1)S(1)}, u32[]{:S(2)}, u32[]{:S(2)}) %collective-permute-start.2) | collective-permute-done | bytes 65568 | tf_op jit(solution)/shard_map/ppermute | solution.py:68
  51.4 2.6 multiply_reduce_fusion.8
  58.4 8.6 %mlp_up.2 = (f32[256,2432]{1,0:T(8,128)}, f32[256,2432]{1,0:T(8,128)}, bf16[256,2432]{1,0:T(8,128)(2,1)}) custom-call(s32[1]{0:T(128)} %bitcast.20.s_ref, bf16[256,448]{1,0:T(8,128)(2,1)} %get-tuple-element.89.bo_ref, bf16[256,448]{1,0:T(8,128)(2,1)} %get-tuple-element.88.bx_ref, bf16[2,448,9728]{2,1,0:T(8,128)(2,1)} %uo_ref.7, ...), custom_call_target="tpu_custom_call" | custom-call | flops 2231369728 | bytes 14500000 | tf_op jit(solution)/shard_map/mlp_up/pallas_call | solution.py:94
  67.0 4.2 fusion.4
  73.9 3.0 convolution_add_fusion
  93.1 2.6 multiply_reduce_fusion.6
  104.9 8.5 %mlp_up.3 = (f32[256,2432]{1,0:T(8,128)}, f32[256,2432]{1,0:T(8,128)}, bf16[256,2432]{1,0:T(8,128)(2,1)}) custom-call(s32[1]{0:T(128)} %bitcast.20.s_ref, bf16[256,448]{1,0:T(8,128)(2,1)} %get-tuple-element.87.bo_ref, bf16[256,448]{1,0:T(8,128)(2,1)} %get-tuple-element.86.bx_ref, bf16[2,448,9728]{2,1,0:T(8,128)(2,1)} %uo_ref.7, ...), custom_call_target="tpu_custom_call" | custom-call | flops 2231369728 | bytes 14500000 | tf_op jit(solution)/shard_map/mlp_up/pallas_call | solution.py:94
  113.5 11.7 %mlp_back.2 = (bf16[256,4864]{1,0:T(8,128)(2,1)}, f32[256,448]{1,0:T(8,128)}, f32[256,448]{1,0:T(8,128)}) custom-call(s32[1]{0:T(128)} %bitcast.20.s_ref, bf16[256,896]{1,0:T(8,128)(2,1)} %pad_maximum_fusion.4.df_ref, bf16[2,2432,896]{2,1,0:T(8,128)(2,1)} %wd_ref.3, f32[256,2432]{1,0:T(8,128)} %get-tuple-element.23.gate_ref, ...), custom_call_target="tpu_custom_call" | custom-call | flops 3347054592 | bytes 23000000 | tf_op jit(solution)/shard_map/mlp_back/pallas_call | solution.py:132
  127.8 3.8 fusion.2
  131.8 3.6 fusion.1
  137.4 3.2 convolution_convert_fusion.7
  147.7 3.1 multiply_reduce_fusion.1
  154.2 11.8 %mlp_back.3 = (bf16[256,4864]{1,0:T(8,128)(2,1)}, f32[256,448]{1,0:T(8,128)}, f32[256,448]{1,0:T(8,128)}) custom-call(s32[1]{0:T(128)} %bitcast.20.s_ref, bf16[256,896]{1,0:T(8,128)(2,1)} %pad_maximum_fusion.5.df_ref, bf16[2,2432,896]{2,1,0:T(8,128)(2,1)} %wd_ref.3, f32[256,2432]{1,0:T(8,128)} %get-tuple-element.27.gate_ref, ...), custom_call_target="tpu_custom_call" | custom-call | flops 3347054592 | bytes 23000000 | tf_op jit(solution)/shard_map/mlp_back/pallas_call | solution.py:132
  175.4 2.5 convolution_convert_fusion.6
  184.0 3.6 fusion
  193.9 8.8 %grad_gu.3 = bf16[448,9728]{1,0:T(8,128)(2,1)} custom-call(s32[1]{0:T(128)} %bitcast.20.s_ref, bf16[2,256,448]{2,1,0:T(8,128)(2,1)} %pad_maximum_fusion.3.b_ref, bf16[256,4864]{1,0:T(8,128)(2,1)} %get-tuple-element.32.own_ref, bf16[256,4864]{1,0:T(8,128)(2,1)} %collective-permute-done.30.oth_ref), custom_call_target="tpu_custom_call" | custom-call | flops 2231369728 | bytes 14000000 | tf_op jit(solution)/shard_map/grad_gu/pallas_call | solution.py:174
  202.7 8.8 %grad_gu.2 = bf16[448,9728]{1,0:T(8,128)(2,1)} custom-call(s32[1]{0:T(128)} %bitcast.20.s_ref, bf16[2,256,448]{2,1,0:T(8,128)(2,1)} %pad_maximum_fusion.2.b_ref, bf16[256,4864]{1,0:T(8,128)(2,1)} %get-tuple-element.31.own_ref, bf16[256,4864]{1,0:T(8,128)(2,1)} %collective-permute-done.29.oth_ref), custom_call_target="tpu_custom_call" | custom-call | flops 2231369728 | bytes 14000000 | tf_op jit(solution)/shard_map/grad_gu/pallas_call | solution.py:174
  218.0 355.5 %all-reduce = (bf16[1,1472]{1,0:T(2,128)(2,1)S(1)}, bf16[1,1472]{1,0:T(2,128)(2,1)S(1)}) all-reduce(bf16[1,1472]{1,0:T(2,128)(2,1)S(1)} %stack.101, bf16[1,1472]{1,0:T(2,128)(2,1)S(1)} %stack.99), channel_id=1, replica_groups=mesh['rep'=64,'shard'=2] {'rep'}, use_global_device_ids=true, to_apply=%region_25.26 | all-reduce | flops 2944 | bytes 11776 | tf_op jit(solution)/shard_map/psum | solution.py:401
  574.8 4.0 maximum_convert_fusion.2
  578.9 3.8 maximum_convert_fusion.3
  582.7 15.1 %maximum_convert_fusion = f32[2,448,9728]{2,1,0:T(8,128)} fusion(bf16[1,448,9728]{2,1,0:T(8,128)(2,1)S(1)} %copy-done.2, bf16[1,448,9728]{2,1,0:T(8,128)(2,1)} %get-tuple-element.60), kind=kLoop, calls=%fused_computation | loop fusion | flops 17432576 | bytes 52297728 | tf_op jit(solution)/shard_map/stack | solution.py:403
  597.8 9.7 %maximum_convert_fusion.1 = f32[2,2432,896]{2,1,0:T(8,128)} fusion(bf16[1,2432,896]{2,1,0:T(8,128)(2,1)S(1)} %bitcast.168, bf16[1,2432,896]{2,1,0:T(8,128)(2,1)} %get-tuple-element.62), kind=kLoop, calls=%fused_computation.1 | loop fusion | flops 8716288 | bytes 26148864 | tf_op jit(solution)/shard_map/stack | solution.py:403
  (385 shorter events, 92.2 us)
Async XLA Ops:
  7.2 567.6 %all-reduce.4.cloned.1.call-start = ((), (), s32[]{:S(2)}) async-start(), calls=%async_computation | async-start | bytes 59637760 | tf_op jit(solution)/shard_map/psum | solution.py:401
  19.1 39.2 %collective-permute-start.5 = (bf16[1,448,9728]{2,1,0:T(8,128)(2,1)}, bf16[1,448,9728]{2,1,0:T(8,128)(2,1)}, u32[]{:S(2)}, u32[]{:S(2)}) collective-permute-start(bf16[1,448,9728]{2,1,0:T(8,128)(2,1)} %get-tuple-element.72), channel_id=1, source_target_pairs={{0,1},{1,0},{2,3},{3,2},{4,5},{5,4},{6,7},{7,6},{8,9},{9,8},{10,11... | collective-permute-start | bytes 26148872 | tf_op jit(solution)/shard_map/ppermute | solution.py:68
  19.3 7.7 %collective-permute-start = (bf16[2,1472]{1,0:T(2,128)(2,1)S(1)}, bf16[2,1472]{1,0:T(2,128)(2,1)S(1)}, u32[]{:S(2)}, u32[]{:S(2)}) collective-permute-start(bf16[2,1472]{1,0:T(2,128)(2,1)S(1)} %concatenate.178), channel_id=1, source_target_pairs={{0,1},{1,0},{2,3},{3,2},{4,5},{5,4},{6,7},{7,6},{8,9},{9,8},{10,11... | collective-permute-start | bytes 17672 | tf_op jit(solution)/shard_map/ppermute | solution.py:68
  21.1 14.8 %collective-permute-start.1 = (bf16[448,1152]{1,0:T(8,128)(2,1)S(1)}, bf16[448,1152]{1,0:T(8,128)(2,1)S(1)}, u32[]{:S(2)}, u32[]{:S(2)}) collective-permute-start(bf16[448,1152]{1,0:T(8,128)(2,1)S(1)} %get-tuple-element.74), channel_id=1, source_target_pairs={{0,1},{1,0},{2,3},{3,2},{4,5},{5,4},{6,7},{7,6},{8,9},{9,8},{10,11... | collective-permute-start | bytes 3096584 | tf_op jit(solution)/shard_map/ppermute | solution.py:68
  22.5 28.9 %collective-permute-start.3 = (bf16[448,896]{1,0:T(8,128)(2,1)}, bf16[448,896]{1,0:T(8,128)(2,1)}, u32[]{:S(2)}, u32[]{:S(2)}) collective-permute-start(bf16[448,896]{1,0:T(8,128)(2,1)} %get-tuple-element.76), channel_id=1, source_target_pairs={{0,1},{1,0},{2,3},{3,2},{4,5},{5,4},{6,7},{7,6},{8,9},{9,8},{10,11... | collective-permute-start | bytes 2408456 | tf_op jit(solution)/shard_map/ppermute | solution.py:68
  23.0 50.9 %collective-permute-start.7 = (bf16[448,1152]{1,0:T(8,128)(2,1)}, bf16[448,1152]{1,0:T(8,128)(2,1)}, u32[]{:S(2)}, u32[]{:S(2)}) collective-permute-start(bf16[448,1152]{1,0:T(8,128)(2,1)} %get-tuple-element.73), channel_id=1, source_target_pairs={{0,1},{1,0},{2,3},{3,2},{4,5},{5,4},{6,7},{7,6},{8,9},{9,8},{10,11... | collective-permute-start | bytes 3096584 | tf_op jit(solution)/shard_map/ppermute | solution.py:68
  27.0 7.9 %collective-permute-start.13 = (bf16[128,896]{1,0:T(8,128)(2,1)S(1)}, bf16[128,896]{1,0:T(8,128)(2,1)S(1)}, u32[]{:S(2)}, u32[]{:S(2)}) collective-permute-start(bf16[128,896]{1,0:T(8,128)(2,1)S(1)} %convert_element_type.170), channel_id=1, source_target_pairs={{0,1},{1,0},{2,3},{3,2},{4,5},{5,4},{6,7},{7,6},{8,9},{9,8},{10,11... | collective-permute-start | bytes 688136 | tf_op jit(solution)/shard_map/ppermute | solution.py:68
  34.9 70.0 %collective-permute-start.11 = (bf16[1,448,9728]{2,1,0:T(8,128)(2,1)}, bf16[1,448,9728]{2,1,0:T(8,128)(2,1)}, u32[]{:S(2)}, u32[]{:S(2)}) collective-permute-start(bf16[1,448,9728]{2,1,0:T(8,128)(2,1)} %get-tuple-element.71), channel_id=1, source_target_pairs={{0,1},{1,0},{2,3},{3,2},{4,5},{5,4},{6,7},{7,6},{8,9},{9,8},{10,11... | collective-permute-start | bytes 26148872 | tf_op jit(solution)/shard_map/ppermute | solution.py:68
  39.6 10.1 %collective-permute-start.2 = (bf16[128,256]{1,0:T(8,128)(2,1)S(1)}, bf16[128,256]{1,0:T(8,128)(2,1)S(1)}, u32[]{:S(2)}, u32[]{:S(2)}) collective-permute-start(bf16[128,256]{1,0:T(8,128)(2,1)S(1)} %pad_maximum_fusion.24), channel_id=1, source_target_pairs={{0,1},{1,0},{2,3},{3,2},{4,5},{5,4},{6,7},{7,6},{8,9},{9,8},{10,11... | collective-permute-start | bytes 196616 | tf_op jit(solution)/shard_map/ppermute | solution.py:68
  49.8 43.3 %collective-permute-start.9 = (bf16[448,896]{1,0:T(8,128)(2,1)}, bf16[448,896]{1,0:T(8,128)(2,1)}, u32[]{:S(2)}, u32[]{:S(2)}) collective-permute-start(bf16[448,896]{1,0:T(8,128)(2,1)} %get-tuple-element.75), channel_id=1, source_target_pairs={{0,1},{1,0},{2,3},{3,2},{4,5},{5,4},{6,7},{7,6},{8,9},{9,8},{10,11... | collective-permute-start | bytes 2408456 | tf_op jit(solution)/shard_map/ppermute | solution.py:68
  56.2 126.3 %collective-permute-start.25 = (bf16[128,448]{1,0:T(8,128)(2,1)}, bf16[128,448]{1,0:T(8,128)(2,1)}, u32[]{:S(2)}, u32[]{:S(2)}) collective-permute-start(bf16[128,448]{1,0:T(8,128)(2,1)} %get-tuple-element.95), channel_id=1, source_target_pairs={{0,1},{1,0},{2,3},{3,2},{4,5},{5,4},{6,7},{7,6},{8,9},{9,8},{10,11... | collective-permute-start | bytes 344072 | tf_op jit(solution)/shard_map/ppermute | solution.py:68
  71.2 2.4 collective-permute-start.6
  83.4 4.5 collective-permute-start.8
  87.8 95.0 %collective-permute-start.24 = (bf16[128,448]{1,0:T(8,128)(2,1)}, bf16[128,448]{1,0:T(8,128)(2,1)}, u32[]{:S(2)}, u32[]{:S(2)}) collective-permute-start(bf16[128,448]{1,0:T(8,128)(2,1)} %get-tuple-element.105), channel_id=1, source_target_pairs={{0,1},{1,0},{2,3},{3,2},{4,5},{5,4},{6,7},{7,6},{8,9},{9,8},{10,11... | collective-permute-start | bytes 344072 | tf_op jit(solution)/shard_map/ppermute | solution.py:68
  96.5 6.2 %collective-permute-start.10 = (bf16[128,896]{1,0:T(8,128)(2,1)}, bf16[128,896]{1,0:T(8,128)(2,1)}, u32[]{:S(2)}, u32[]{:S(2)}) collective-permute-start(bf16[128,896]{1,0:T(8,128)(2,1)} %multiply_convert_fusion), channel_id=1, source_target_pairs={{0,1},{1,0},{2,3},{3,2},{4,5},{5,4},{6,7},{7,6},{8,9},{9,8},{10,11... | collective-permute-start | bytes 688136 | tf_op jit(solution)/shard_map/ppermute | solution.py:68
  102.6 67.9 %collective-permute-start.27 = (bf16[128,448]{1,0:T(8,128)(2,1)}, bf16[128,448]{1,0:T(8,128)(2,1)}, u32[]{:S(2)}, u32[]{:S(2)}) collective-permute-start(bf16[128,448]{1,0:T(8,128)(2,1)} %get-tuple-element.97), channel_id=1, source_target_pairs={{0,1},{1,0},{2,3},{3,2},{4,5},{5,4},{6,7},{7,6},{8,9},{9,8},{10,11... | collective-permute-start | bytes 344072 | tf_op jit(solution)/shard_map/ppermute | solution.py:68
  127.1 8.3 %collective-permute-start.14 = (f32[128,896]{1,0:T(8,128)S(1)}, f32[128,896]{1,0:T(8,128)S(1)}, u32[]{:S(2)}, u32[]{:S(2)}) collective-permute-start(f32[128,896]{1,0:T(8,128)S(1)} %slice.428), channel_id=1, source_target_pairs={{0,1},{1,0},{2,3},{3,2},{4,5},{5,4},{6,7},{7,6},{8,9},{9,8},{10,11... | collective-permute-start | bytes 1376264 | tf_op jit(solution)/shard_map/ppermute | solution.py:68
  131.7 3.9 collective-permute-start.12
  168.0 5.5 collective-permute-start.17
  170.5 23.4 %collective-permute-start.30 = (bf16[256,4864]{1,0:T(8,128)(2,1)}, bf16[256,4864]{1,0:T(8,128)(2,1)}, u32[]{:S(2)}, u32[]{:S(2)}) collective-permute-start(bf16[256,4864]{1,0:T(8,128)(2,1)} %get-tuple-element.32.own_ref), channel_id=1, source_target_pairs={{0,1},{1,0},{2,3},{3,2},{4,5},{5,4},{6,7},{7,6},{8,9},{9,8},{10,11... | collective-permute-start | bytes 7471112 | tf_op jit(solution)/shard_map/ppermute | solution.py:68
  173.4 29.3 %collective-permute-start.29 = (bf16[256,4864]{1,0:T(8,128)(2,1)}, bf16[256,4864]{1,0:T(8,128)(2,1)}, u32[]{:S(2)}, u32[]{:S(2)}) collective-permute-start(bf16[256,4864]{1,0:T(8,128)(2,1)} %get-tuple-element.31.own_ref), channel_id=1, source_target_pairs={{0,1},{1,0},{2,3},{3,2},{4,5},{5,4},{6,7},{7,6},{8,9},{9,8},{10,11... | collective-permute-start | bytes 7471112 | tf_op jit(solution)/shard_map/ppermute | solution.py:68
  182.6 9.8 %collective-permute-start.23 = (bf16[128,448]{1,0:T(8,128)(2,1)S(1)}, bf16[128,448]{1,0:T(8,128)(2,1)S(1)}, u32[]{:S(2)}, u32[]{:S(2)}) collective-permute-start(bf16[128,448]{1,0:T(8,128)(2,1)S(1)} %copy-done.49), channel_id=1, source_target_pairs={{0,1},{1,0},{2,3},{3,2},{4,5},{5,4},{6,7},{7,6},{8,9},{9,8},{10,11... | collective-permute-start | bytes 344072 | tf_op jit(solution)/shard_map/ppermute | solution.py:68
  182.8 7.3 %collective-permute-start.26 = (bf16[128,896]{1,0:T(8,128)(2,1)S(1)}, bf16[128,896]{1,0:T(8,128)(2,1)S(1)}, u32[]{:S(2)}, u32[]{:S(2)}) collective-permute-start(bf16[128,896]{1,0:T(8,128)(2,1)S(1)} %copy-done.44), channel_id=1, source_target_pairs={{0,1},{1,0},{2,3},{3,2},{4,5},{5,4},{6,7},{7,6},{8,9},{9,8},{10,11... | collective-permute-start | bytes 688136 | tf_op jit(solution)/shard_map/ppermute | solution.py:68
  183.6 8.7 %collective-permute-start.20 = (bf16[128,1152]{0,1:T(8,128)(2,1)S(1)}, bf16[128,1152]{0,1:T(8,128)(2,1)S(1)}, u32[]{:S(2)}, u32[]{:S(2)}) collective-permute-start(bf16[128,1152]{0,1:T(8,128)(2,1)S(1)} %pad_maximum_fusion.7), channel_id=1, source_target_pairs={{0,1},{1,0},{2,3},{3,2},{4,5},{5,4},{6,7},{7,6},{8,9},{9,8},{10,11... | collective-permute-start | bytes 884744 | tf_op jit(solution)/shard_map/ppermute | solution.py:68
  (88 other events, 482.7 us)
Sparse Core Ops, SparseCore 0:
  211.7 310.3 all-reduce.3
